TPU v7x, 128 devices: a whole 4x4x4 slice. The times are simulated.
128 devices in a mesh: src: 4 (over x), tile: 32 (over z, y, core).
Axes of the slice: x: 4, y: 4, z: 4, core: 2. Of those that a mesh axis runs over, the one named last changes fastest.
Arguments:
- latent: bfloat16 [3, 128, 16, 160], P(None, ('src', 'tile')), may hold values from -6 to 6
- row_map: int32 [128], replicated, may hold values from 0 to 127, each once
- latent_cache: bfloat16 [2, 128, 16, 160], P(None, 'tile'), may hold values from -6 to 6
- cache_one: bfloat16 [2, 128, 384, 160], P(None, 'tile', 'src'), may hold values from -5 to 5
- cache_two: bfloat16 [2, 128, 384, 160], P(None, 'tile', 'src'), may hold values from -5 to 5
- conv_in_w: bfloat16 [3, 3, 3, 16, 384], P(None, None, None, None, 'src'), may hold values from -0.3125 to 0.3125
- weight_one: bfloat16 [3, 3, 3, 384, 384], P(None, None, None, 'src'), may hold values from -0.0625 to 0.0625
- weight_two: bfloat16 [3, 3, 3, 384, 384], P(None, None, None, 'src'), may hold values from -0.0625 to 0.0625
- gain_one: float32 [384], P('src'), may hold values from 0.1 to 1.9
- gain_two: float32 [384], P('src'), may hold values from 0.1 to 1.9
Outputs:
- decoded: bfloat16 [3, 128, 384, 160], P(None, 'tile', 'src')
All inputs are finite; a program needn't handle non-finite values.
Results may differ from a plain program's by a relative error of at most 0.0037.
The roundings to bfloat16 on the way count: a program that leaves them out, or rounds other values in their place, can miss the bound.
Values may be sent and summed in bfloat16 or wider, within the bound.
A program may use at most 128 MiB of HBM per device.

v0:
```python
import functools

import jax
import jax.numpy as jnp
from jax import lax
from jax.experimental import pallas as pl
from jax.experimental.pallas import tpu as pltpu
from jax.sharding import Mesh
from jax.sharding import PartitionSpec as P

GSIZE = 12
GROUPS = 32
AXES = ("src", "z", "y", "core")
TILE = ("z", "y", "core")
SIZES = (4, 4, 4, 2)
MESH = pl.DeviceIdType.MESH
F32 = jnp.float32
BF16 = jnp.bfloat16

TAIL, UP_MAIN, UP_TAIL, DOWN_TAIL, DOWN_MAIN = 3, 5, 6, 7, 8
ROW_SLOT = (4, 0, 1, 2)
SLOT_OF = (UP_MAIN, 4, 0, 1, 2, DOWN_MAIN)
PLANE = tuple((z, y) for z in range(4) for y in range(4) if z or y)


def dot(a, b):
    return lax.dot_general(a, b, (((1,), (0,)), ((), ())), preferred_element_type=F32)


def dot_exact(a, b, dims):
    return lax.dot_general(
        a, b, (dims, ((), ())), precision=lax.Precision.HIGHEST, preferred_element_type=F32
    )


def iota(shape, dim):
    return lax.broadcasted_iota(jnp.int32, shape, dim)


def body(
    entries,
    index_ref,
    latent_ref,
    lcache_ref,
    win_ref,
    gains_ref,
    cache1_hbm,
    cache2_hbm,
    w1_hbm,
    w2_hbm,
    out_ref,
    units,
    rows_all,
    picked,
    lcache,
    shifted,
    win,
    gains,
    stage1,
    stage2,
    w1,
    w2,
    x1,
    x2,
    t1,
    t2,
    acc,
    kept,
    sum1,
    sum2,
    mean_ref,
    scale_ref,
    stat,
    stat_core,
    stat_src,
    send_sem,
    recv_sem,
    local_sem,
):
    s, z, y, core = (lax.axis_index(a) for a in AXES)
    tile = z * 8 + y * 2 + core
    plane = z * 4 + y
    own = pl.ds(pl.multiple_of(s * 96, 96), 96)
    nxt, prv = lax.rem(tile + 1, 32), lax.rem(tile + 31, 32)

    def at_tile(t):
        return (s, t // 8, lax.rem(t // 2, 4), lax.rem(t, 2))

    def src_peer(d):
        return (lax.rem(s + d, 4), z, y, core)

    def plane_peer(k):
        dz, dy = PLANE[k]
        return (s, lax.rem(z + dz, 4), lax.rem(y + dy, 4), core)

    other = (s, z, y, 1 - core)
    counter = [0]

    def remote(src, dst, device):
        k = counter[0]
        counter[0] += 1
        c = pltpu.make_async_remote_copy(
            src_ref=src,
            dst_ref=dst,
            send_sem=send_sem.at[k],
            recv_sem=recv_sem.at[k],
            device_id=device,
            device_id_type=MESH,
        )
        c.start()
        return c

    def local(src, dst, k):
        c = pltpu.make_async_copy(src, dst, local_sem.at[k])
        c.start()
        return c

    sent = []

    def arrived(copies):
        for c in copies:
            c.wait_recv()
        sent.extend(copies)

    def gone():
        for c in sent:
            c.wait_send()
        sent.clear()

    barrier = pltpu.get_barrier_semaphore()
    peers = [src_peer(d) for d in (1, 2, 3)] + [plane_peer(k) for k in range(15)]
    peers += [other, at_tile(nxt), at_tile(prv)]
    for p in peers:
        pl.semaphore_signal(barrier, inc=1, device_id=p, device_id_type=MESH)
    c1 = local(cache1_hbm, stage1, 0)
    c2 = local(cache2_hbm, stage2, 1)
    wl1 = [
        local(w1_hbm.at[:, b], w1.at[:, :, :, pl.ds(b * 384, 384)], 2 + b) for b in range(3)
    ]
    wl2 = [
        local(w2_hbm.at[:, b], w2.at[:, :, :, pl.ds(b * 384, 384)], 5 + b) for b in range(3)
    ]

    from_col, to_col = iota((160, 128), 0), iota((160, 128), 1)

    def tail_place(k):
        hit = (from_col >= 128) & (from_col - 128 == to_col - 32 * k)
        return jnp.where(hit, 1.0, 0.0).astype(BF16)

    place = [tail_place(k) for k in range(4)]

    for f in range(3):
        units[f] = latent_ref[f, :, 0:128]
    tails = sum(dot(latent_ref[f], place[f]) for f in range(3))
    units[3] = tails.astype(BF16)
    base = pl.multiple_of(core * 64 + plane * 4, 4)
    rows_all[base + s] = units[s]
    win[own] = win_ref[...]
    gains[own] = gains_ref[...]
    for f in range(2):
        lcache[f, 2:6] = lcache_ref[f]
    pl.semaphore_wait(barrier, len(peers))

    step0 = [
        remote(units.at[lax.rem(s + d, 4)], rows_all.at[base + s], src_peer(d)) for d in (1, 2, 3)
    ]
    edges = [
        remote(lcache_ref.at[:, 2:4], lcache.at[:, 0:2], at_tile(nxt)),
        remote(lcache_ref.at[:, 0:2], lcache.at[:, 6:8], at_tile(prv)),
    ]
    params = [remote(win_ref, win.at[own], src_peer(d)) for d in (1, 2, 3)]
    params += [remote(gains_ref, gains.at[own], src_peer(d)) for d in (1, 2, 3)]

    def pack_cache(staged, x):
        for f in range(2):
            total = jnp.zeros((96, 128), F32)
            for h in range(4):
                x[f, ROW_SLOT[h], own] = staged[f, h, :, 0:128]
                total = total + dot(staged[f, h], place[h])
            x[f, TAIL, own] = total.astype(BF16)

    def spread(x, frames):
        block = x.at[frames, 0:5, own]
        return [remote(block, block, src_peer(d)) for d in (1, 2, 3)]

    def halo(x, frames):
        return [
            remote(x.at[frames, 2:4], x.at[frames, 5:7], at_tile(nxt)),
            remote(x.at[frames, 3:5], x.at[frames, 7:9], at_tile(prv)),
        ]

    c1.wait()
    pack_cache(stage1, x1)
    arrived(step0)
    mine = rows_all.at[pl.ds(base, 4)]
    step1 = [remote(mine, mine, plane_peer(k)) for k in range(15)]
    cached1 = spread(x1, pl.ds(0, 2))
    c2.wait()
    pack_cache(stage2, x2)

    wide_from, wide_to = iota((160, 256), 0), iota((160, 256), 1)
    shift = jnp.concatenate(
        [jnp.where(wide_from == wide_to + e - 1, 1.0, 0.0).astype(BF16) for e in range(3)], axis=1
    )
    image_row = tile * 4 - 2 + iota((8, 16, 256), 0)
    in_image = (image_row >= 0) & (image_row < 128)

    def put_shifted(f, wide):
        for e in range(3):
            part = wide[:, e * 256 : (e + 1) * 256].reshape(8, 16, 256)
            shifted[f, :, e * 16 : (e + 1) * 16] = jnp.where(in_image, part, 0.0).astype(BF16)

    arrived(edges)
    for f in range(2):
        put_shifted(f, dot(lcache[f].reshape(128, 160), shift))

    arrived(step1)
    half = rows_all.at[pl.ds(pl.multiple_of(core * 64, 64), 64)]
    step2 = [remote(half, half, other)]
    arrived(step2)
    for j in range(8):
        picked[s, j] = rows_all[index_ref[j]]
    step3 = [remote(picked.at[s], picked.at[s], src_peer(d)) for d in (1, 2, 3)]
    arrived(params)
    arrived(step3)
    cached2 = spread(x2, pl.ds(0, 2))
    tail_from, tail_to = iota((128, 256), 0), iota((128, 256), 1)
    for f in range(3):
        tail_shift = []
        for e in range(3):
            j = tail_from - 32 * f
            hit = (j >= 0) & (j < 32) & (128 + j == tail_to + e - 1)
            tail_shift.append(jnp.where(hit, 1.0, 0.0).astype(BF16))
        wide = dot(picked[f].reshape(128, 128), shift[0:128]) + dot(
            picked[3].reshape(128, 128), jnp.concatenate(tail_shift, axis=1)
        )
        put_shifted(2 + f, wide)

    lane = iota((384, 128), 1)
    lane96 = iota((96, 128), 1)
    sum1[...] = jnp.zeros_like(sum1)
    sum2[...] = jnp.zeros_like(sum2)

    @pl.loop(0, 3)
    def _(t):
        tail = jnp.zeros((384, 128), F32)
        for h in range(6):
            window = jnp.concatenate(
                [shifted[t + a, h : h + 3].reshape(144, 256) for a in range(3)], axis=0
            )
            got = dot(win[...], window)
            first = got[:, 0:128].astype(BF16)
            x1[t + 2, SLOT_OF[h]] = first
            ends = got[:, 128:256]
            if h == 0:
                x1[t + 2, UP_TAIL] = pltpu.roll(ends, 96, 1).astype(BF16)
            elif h == 5:
                x1[t + 2, DOWN_TAIL] = ends.astype(BF16)
            else:
                if h > 1:
                    ends = pltpu.roll(ends, 32 * (h - 1), 1)
                hit = (lane >= 32 * (h - 1)) & (lane < 32 * h)
                tail = jnp.where(hit, ends, tail)
                full = first.astype(F32)
                sum1[...] += full
                sum2[...] += full * full
        tail = tail.astype(BF16)
        x1[t + 2, TAIL] = tail
        full = tail.astype(F32)
        sum1[...] += full
        sum2[...] += full * full

    for t in range(3):
        kept[t] = x1[t + 2, 0:5, own]

    channel, group = iota((384, 128), 0), iota((384, 128), 1)

    def member(first_lane):
        low = (group - first_lane) * GSIZE
        hit = (channel >= low) & (channel < low + GSIZE)
        return jnp.where(hit & (group >= first_lane) & (group < first_lane + 32), 1.0, 0.0)

    def stat_row(a, b, rows):
        ones = jnp.ones((8, 128), F32)
        ra = dot_exact(ones, a, ((1,), (1,)))
        rb = dot_exact(ones, b, ((1,), (1,)))
        return ra, rb

    def share_stats(k):
        mine = stat.at[k, core, plane]
        return [remote(mine, mine, plane_peer(i)) for i in range(15)]

    def share_core(k):
        total = stat[k, core, 0]
        for i in range(1, 16):
            total = total + stat[k, core, i]
        stat_core[k, core] = total
        mine = stat_core.at[k, core]
        return [remote(mine, mine, other)]

    def coefficients(total, column):
        mean = total / entries
        square = pltpu.roll(mean, 96, 1)
        spread_ = jnp.maximum(square - mean * mean, 0.0)
        rstd = lax.rsqrt(spread_ + 1e-06)
        one = member(0)
        mean_c = jnp.sum(one * mean[0:1], axis=1, keepdims=True)
        rstd_c = jnp.sum(one * rstd[0:1], axis=1, keepdims=True)
        mean_ref[...] = jnp.broadcast_to(mean_c, (384, 128))
        scale = rstd_c * gains[:, column : column + 1] * 0.5
        scale_ref[...] = jnp.broadcast_to(scale, (384, 128))

    def prepare(x, t, f, norm):
        no_up = jnp.where(tile == 0, 128, 0)
        no_down = jnp.where(tile == 31, 128, 0)
        down_limit = jnp.where(tile == 31, 32, 0)
        up_limit = jnp.where(tile == 0, 96, 128)

        @pl.loop(0, 4)
        def _(c):
            part = pl.ds(pl.multiple_of(c * 96, 96), 96)
            mean, scale = mean_ref[part], scale_ref[part]

            def act(v):
                v = v.astype(F32)
                if not norm:
                    return v
                u = (v - mean) * scale
                return u + u * jnp.tanh(u)

            if norm:
                for slot in ROW_SLOT:
                    x[f, slot, part] = act(x[f, slot, part]).astype(BF16)
            up = act(x[f, UP_MAIN, part])
            x[f, UP_MAIN, part] = jnp.where(lane96 < no_up, 0.0, up).astype(BF16)
            down = act(x[f, DOWN_MAIN, part])
            x[f, DOWN_MAIN, part] = jnp.where(lane96 < no_down, 0.0, down).astype(BF16)
            mid = act(x[f, TAIL, part])
            rim = jnp.where(
                lane96 < 32,
                x[f, DOWN_TAIL, part].astype(F32),
                x[f, UP_TAIL, part].astype(F32),
            )
            rim = act(rim)
            rim = jnp.where((lane96 < down_limit) | (lane96 >= up_limit), 0.0, rim)
            t[f, 1, part] = mid.astype(BF16)
            t[f, 0, part] = pltpu.roll(jnp.where(lane96 >= 96, rim, mid), 32, 1).astype(BF16)
            t[f, 2, part] = pltpu.roll(jnp.where(lane96 < 32, rim, mid), 96, 1).astype(BF16)

    def conv_frame(x, t, w, f):
        low, high = max(0, f - 2), min(2, f)
        count = high - low + 1
        taps = w[low : high + 1].reshape(count * 288, 1152)

        def add(got, i):
            for n, a in enumerate(range(low, high + 1)):
                part = got[n * 288 : (n + 1) * 288]
                if a == 0:
                    acc[f - a, i] = part
                else:
                    acc[f - a, i] += part

        def rows(h):
            return jnp.concatenate([x[f, SLOT_OF[h + b]] for b in range(3)], axis=0)

        for p in range(2):
            got = dot(taps, jnp.concatenate([rows(2 * p), rows(2 * p + 1)], axis=1))
            add(got[:, 0:128], 2 * p)
            add(got[:, 128:256], 2 * p + 1)
        add(dot(taps, t[f].reshape(1152, 128)), 4)

    def combined(t):
        def a(i, e):
            return acc[t, i, e * 96 : (e + 1) * 96]

        before = [pltpu.roll(a(h, 0), 1, 1) for h in range(4)]
        mains = []
        for h in range(4):
            after = jnp.where(
                lane96 == 127, pltpu.roll(a(4, 2), 127 - 32 * h, 1), pltpu.roll(a(h, 2), 127, 1)
            )
            mains.append(a(h, 1) + jnp.where(lane96 == 0, 0.0, before[h]) + after)
        left = pltpu.roll(a(4, 0), 1, 1)
        for h in range(4):
            moved = before[h] if h == 0 else pltpu.roll(before[h], 32 * h, 1)
            left = jnp.where(lane96 == 32 * h, moved, left)
        right = jnp.where((lane96 & 31) == 31, 0.0, pltpu.roll(a(4, 2), 127, 1))
        return mains, a(4, 1) + left + right

    ra, rb = stat_row(sum1[...], sum2[...], 384)
    stat[0, core, plane] = dot_exact(ra, member(0), ((1,), (0,))) + dot_exact(
        rb, member(32), ((1,), (0,))
    )
    shared = share_stats(0)
    arrived(cached1)
    rims = halo(x1, pl.ds(0, 2))
    arrived(shared)
    shared = share_core(0)
    for c in wl1:
        c.wait()
    arrived(rims)
    prepare(x1, t1, 0, False)
    prepare(x1, t1, 1, False)
    conv_frame(x1, t1, w1, 0)
    conv_frame(x1, t1, w1, 1)
    arrived(shared)
    coefficients(stat_core[0, 0] + stat_core[0, 1], 0)

    total1 = jnp.zeros((96, 128), F32)
    total2 = jnp.zeros((96, 128), F32)
    middles = []
    for t in range(3):
        prepare(x1, t1, t + 2, True)
        conv_frame(x1, t1, w1, t + 2)
        mains, tail = combined(t)
        for h in range(4):
            x2[t + 2, ROW_SLOT[h], own] = mains[h].astype(BF16)
        x2[t + 2, TAIL, own] = tail.astype(BF16)
        for v in mains + [tail]:
            total1 = total1 + v
            total2 = total2 + v * v
        middles.append(spread(x2, t + 2))

    ones = jnp.ones((8, 128), F32)
    sum1[...] = jnp.zeros_like(sum1)
    sum2[...] = jnp.zeros_like(sum2)
    sum1[own] = total1
    sum2[own] = total2
    ra, rb = stat_row(sum1[...], sum2[...], 384)
    stat[1, core, plane] = dot_exact(ra, member(0), ((1,), (0,))) + dot_exact(
        rb, member(32), ((1,), (0,))
    )
    shared = share_stats(1)
    arrived(cached2)
    rims2 = halo(x2, pl.ds(0, 2))
    arrived(shared)
    shared = share_core(1)
    for c in wl2:
        c.wait()
    arrived(rims2)
    prepare(x2, t2, 0, False)
    arrived(shared)
    stat_src[s] = stat_core[1, 0] + stat_core[1, 1]
    shared = [remote(stat_src.at[s], stat_src.at[s], src_peer(d)) for d in (1, 2, 3)]
    arrived(middles[0])
    rims = [halo(x2, 2)]
    prepare(x2, t2, 1, False)
    conv_frame(x2, t2, w2, 0)
    arrived(middles[1])
    rims.append(halo(x2, 3))
    conv_frame(x2, t2, w2, 1)
    arrived(shared)
    coefficients(stat_src[0] + stat_src[1] + stat_src[2] + stat_src[3], 1)
    for t in range(3):
        arrived(rims[t])
        gone()
        prepare(x2, t2, t + 2, True)
        conv_frame(x2, t2, w2, t + 2)
        if t == 0:
            arrived(middles[2])
            rims.append(halo(x2, 4))
        mains, tail = combined(t)
        for h in range(4):
            out = kept[t, ROW_SLOT[h]].astype(F32) + mains[h]
            out_ref[t, h, :, 0:128] = out.astype(BF16)
        out = kept[t, TAIL].astype(F32) + tail
        for h in range(4):
            moved = out if h == 0 else pltpu.roll(out, 128 - 32 * h, 1)
            out_ref[t, h, :, 128:160] = moved[:, 0:32].astype(BF16)
    gone()


def per_device(
    latent,
    row_map,
    latent_cache,
    cache_one,
    cache_two,
    conv_in_w,
    weight_one,
    weight_two,
    gain_one,
    gain_two,
):
    frames, _, channels_in, columns = latent.shape
    tile = lax.axis_index(TILE)
    wanted = jnp.clip(tile * 4 - 2 + jnp.arange(8, dtype=jnp.int32), 0, 127)
    places = jnp.arange(128, dtype=jnp.int32)
    t = places % 32
    slot = (t % 2) * 64 + (t // 2) * 4 + places // 32
    index = jnp.sum(
        jnp.where(row_map[None, :] == wanted[:, None], slot[None, :], 0), axis=1, dtype=jnp.int32
    )
    win = conv_in_w.reshape(27 * channels_in, -1).T
    gains = jnp.pad(jnp.stack([gain_one, gain_two], axis=1), ((0, 0), (0, 126)))
    entries = float(frames * 128 * GSIZE * columns)
    vmem = pl.BlockSpec(memory_space=pltpu.VMEM)
    hbm = pl.BlockSpec(memory_space=pl.ANY)
    smem = pl.BlockSpec(memory_space=pltpu.SMEM)
    copies = 3 + 2 + 6 + 15 + 1 + 3 + 3 + 3 + 15 + 2 + 1 + 9 + 15 + 2 + 1 + 3 + 6
    return pl.pallas_call(
        functools.partial(body, entries),
        out_shape=jax.ShapeDtypeStruct((3, 4, 96, 160), BF16),
        in_specs=[smem, vmem, vmem, vmem, vmem, hbm, hbm, hbm, hbm],
        out_specs=vmem,
        scratch_shapes=[
            pltpu.VMEM((4, 16, 128), BF16),
            pltpu.VMEM((128, 16, 128), BF16),
            pltpu.VMEM((4, 8, 16, 128), BF16),
            pltpu.VMEM((2, 8, 16, 160), BF16),
            pltpu.VMEM((5, 8, 48, 256), BF16),
            pltpu.VMEM((384, 432), BF16),
            pltpu.VMEM((384, 128), F32),
            pltpu.VMEM((2, 4, 96, 160), BF16),
            pltpu.VMEM((2, 4, 96, 160), BF16),
            pltpu.VMEM((3, 3, 96, 1152), BF16),
            pltpu.VMEM((3, 3, 96, 1152), BF16),
            pltpu.VMEM((5, 9, 384, 128), BF16),
            pltpu.VMEM((5, 9, 384, 128), BF16),
            pltpu.VMEM((5, 3, 384, 128), BF16),
            pltpu.VMEM((5, 3, 384, 128), BF16),
            pltpu.VMEM((3, 5, 288, 128), F32),
            pltpu.VMEM((3, 5, 96, 128), BF16),
            pltpu.VMEM((384, 128), F32),
            pltpu.VMEM((384, 128), F32),
            pltpu.VMEM((384, 128), F32),
            pltpu.VMEM((384, 128), F32),
            pltpu.VMEM((2, 2, 16, 8, 128), F32),
            pltpu.VMEM((2, 2, 8, 128), F32),
            pltpu.VMEM((4, 8, 128), F32),
            pltpu.SemaphoreType.DMA((copies,)),
            pltpu.SemaphoreType.DMA((copies,)),
            pltpu.SemaphoreType.DMA((8,)),
        ],
        compiler_params=pltpu.CompilerParams(
            collective_id=0, has_side_effects=True, vmem_limit_bytes=56 << 20
        ),
    )(
        index,
        latent.reshape(frames, channels_in, columns),
        latent_cache,
        win,
        gains,
        cache_one,
        cache_two,
        weight_one,
        weight_two,
    )


def solution(mesh):
    torus = Mesh(mesh.devices.reshape(SIZES), AXES)
    all_axes = ("src",) + TILE
    in_specs = (
        P(None, all_axes, None, None),
        P(),
        P(None, TILE, None, None),
        P(None, TILE, "src", None),
        P(None, TILE, "src", None),
        P(None, None, None, None, "src"),
        P(None, None, None, "src", None),
        P(None, None, None, "src", None),
        P("src"),
        P("src"),
    )
    return jax.shard_map(
        per_device,
        mesh=torus,
        in_specs=in_specs,
        out_specs=P(None, TILE, "src", None),
        check_vma=False,
    )
```

profile of v0, /device:TPU:0, one launch (start us, length us, event | category | flops | bytes accessed | tf_op | source)
XLA Modules:
  0.0 91.1 jit_solution(342752720287138033)
XLA Ops:
  0.0 1.4 %select_reduce_fusion.index_ref = s32[8]{0:T(128)} fusion(s32[128]{0:T(128)S(1)} %fusion, s32[128]{0:T(128)} %param.11, s32[8]{0:T(128)S(1)} %add_clamp_fusion), kind=kLoop, calls=%fused_computation | loop fusion | flops 3064 | bytes 1088 | tf_op jit(solution)/shard_map/reduce_sum | solution.py:491
  1.4 0.7 pad_maximum_fusion
  2.1 0.1 copy.29
  2.2 0.6 pad.4.gains_ref
  2.9 1.6 %copy.28 = bf16[432,96]{0,1:T(8,128)(2,1)} copy(bf16[432,96]{1,0:T(8,128)(2,1)} %bitcast.6) | data formatting | bytes 165888 | tf_op jit(solution)/shard_map/reshape | solution.py:494
  4.5 1.9 %copy.30.cache1_hbm = bf16[2,4,96,160]{3,2,1,0:T(8,128)(2,1)} copy(bf16[2,4,96,160]{2,3,1,0:T(8,128)(2,1)} %param.13) | data formatting | bytes 491520 | tf_op args[3]
  6.4 1.9 %copy.31.cache2_hbm = bf16[2,4,96,160]{3,2,1,0:T(8,128)(2,1)} copy(bf16[2,4,96,160]{2,3,1,0:T(8,128)(2,1)} %param.14) | data formatting | bytes 491520 | tf_op args[4]
  8.3 80.7 %shard_map.100 = bf16[3,4,96,160]{3,2,1,0:T(8,128)(2,1)} custom-call(s32[8]{0:T(128)} %select_reduce_fusion.index_ref, bf16[3,16,160]{2,1,0:T(8,128)(2,1)} %bitcast.7, bf16[2,4,16,160]{3,2,1,0:T(8,128)(2,1)} %lcache_ref.1, bf16[96,432]{1,0:T(8,128)(2,1)} %bitcast.5, f32[96,128]{1,0:T(8,128)} %pad.4.gains_ref, bf16[2,4,96,160]{3,2,1,0:T(8,128)(2,1)} %copy.30.cache1_hbm, ...), custom_call_target="tpu_custom_call" | custom-call | tf_op jit(solution)/shard_map/pallas_call | solution.py:501
  89.0 2.1 %copy.32 = bf16[3,4,96,160]{2,3,1,0:T(8,128)(2,1)} copy(bf16[3,4,96,160]{3,2,1,0:T(8,128)(2,1)} %shard_map.100) | data formatting | bytes 737280 | tf_op jit(solution)/shard_map/pallas_call | solution.py:501
  (2 shorter events, 0.0 us)
where the time goes:
time: 91.4 us; the launch traced here: 91.1 us
  Pallas kernels  80.7 us (88%)
  local copies, waits for them, and re-layouts  8.3 us (9%)
  other arithmetic  2.11 us (2%)
    pallas_call x1, Pallas kernels, per_device(): pl.pallas_call(functools.partial(body, entries), out_shape=jax.ShapeDtype...  80.7 us
    unnamed x2, local copies, waits for them, and re-layouts  3.83 us
    pallas_call x1, local copies, waits for them, and re-layouts, per_device(): pl.pallas_call(functools.partial(body, entries), out_shape=jax.ShapeDtype...  2.1 us

commit v1 on v0

--- a/solution.py
+++ b/solution.py
@@ -27,6 +27,10 @@
     return lax.dot_general(a, b, (((1,), (0,)), ((), ())), preferred_element_type=F32)
 
 
+def dot_t(a, b):
+    return lax.dot_general(a, b, (((1,), (1,)), ((), ())), preferred_element_type=F32)
+
+
 def dot_exact(a, b, dims):
     return lax.dot_general(
         a, b, (dims, ((), ())), precision=lax.Precision.HIGHEST, preferred_element_type=F32
@@ -39,11 +43,12 @@
 
 def body(
     entries,
-    index_ref,
+    map_ref,
     latent_ref,
     lcache_ref,
     win_ref,
-    gains_ref,
+    gain1_ref,
+    gain2_ref,
     cache1_hbm,
     cache2_hbm,
     w1_hbm,
@@ -56,6 +61,7 @@
     shifted,
     win,
     gains,
+    choice,
     stage1,
     stage2,
     w1,
@@ -71,8 +77,7 @@
     mean_ref,
     scale_ref,
     stat,
-    stat_core,
-    stat_src,
+    stat_ring,
     send_sem,
     recv_sem,
     local_sem,
@@ -94,6 +99,12 @@
         return (s, lax.rem(z + dz, 4), lax.rem(y + dy, 4), core)
 
     other = (s, z, y, 1 - core)
+
+    def ring_peer(i):
+        if i < 3:
+            return src_peer(i + 1)
+        return (lax.rem(s + i - 3, 4), z, y, 1 - core)
+
     counter = [0]
 
     def remote(src, dst, device):
@@ -129,7 +140,7 @@
 
     barrier = pltpu.get_barrier_semaphore()
     peers = [src_peer(d) for d in (1, 2, 3)] + [plane_peer(k) for k in range(15)]
-    peers += [other, at_tile(nxt), at_tile(prv)]
+    peers += [ring_peer(i) for i in range(3, 7)] + [at_tile(nxt), at_tile(prv)]
     for p in peers:
         pl.semaphore_signal(barrier, inc=1, device_id=p, device_id_type=MESH)
     c1 = local(cache1_hbm, stage1, 0)
@@ -147,7 +158,7 @@
         hit = (from_col >= 128) & (from_col - 128 == to_col - 32 * k)
         return jnp.where(hit, 1.0, 0.0).astype(BF16)
 
-    place = [tail_place(k) for k in range(4)]
+    place = [tail_place(k) for k in range(3)]
 
     for f in range(3):
         units[f] = latent_ref[f, :, 0:128]
@@ -155,10 +166,24 @@
     units[3] = tails.astype(BF16)
     base = pl.multiple_of(core * 64 + plane * 4, 4)
     rows_all[base + s] = units[s]
-    win[own] = win_ref[...]
-    gains[own] = gains_ref[...]
+    eye = jnp.where(iota((96, 96), 0) == iota((96, 96), 1), 1.0, 0.0).astype(BF16)
+    taps_in = dot_t(eye, win_ref[...]).astype(BF16)
+    win[0, s] = taps_in[0:48]
+    win[1, s] = taps_in[48:96]
+    gains[s] = jnp.zeros((8, 128), F32)
+    gains[s, 0:1, 0:96] = gain1_ref[...]
+    gains[s, 1:2, 0:96] = gain2_ref[...]
     for f in range(2):
         lcache[f, 2:6] = lcache_ref[f]
+    def pack_cache(staged, x):
+        for f in range(2):
+            for h in range(4):
+                x[f, ROW_SLOT[h], own] = dot_t(eye, staged[f, h, 0:128]).astype(BF16)
+            tails = jnp.concatenate([staged[f, h, 128:160] for h in range(4)], axis=0)
+            x[f, TAIL, own] = dot_t(eye, tails).astype(BF16)
+
+    c1.wait()
+    pack_cache(stage1, x1)
     pl.semaphore_wait(barrier, len(peers))
 
     step0 = [
@@ -168,20 +193,19 @@
         remote(lcache_ref.at[:, 2:4], lcache.at[:, 0:2], at_tile(nxt)),
         remote(lcache_ref.at[:, 0:2], lcache.at[:, 6:8], at_tile(prv)),
     ]
-    params = [remote(win_ref, win.at[own], src_peer(d)) for d in (1, 2, 3)]
-    params += [remote(gains_ref, gains.at[own], src_peer(d)) for d in (1, 2, 3)]
-
-    def pack_cache(staged, x):
-        for f in range(2):
-            total = jnp.zeros((96, 128), F32)
-            for h in range(4):
-                x[f, ROW_SLOT[h], own] = staged[f, h, :, 0:128]
-                total = total + dot(staged[f, h], place[h])
-            x[f, TAIL, own] = total.astype(BF16)
+    params = [remote(gains.at[s], gains.at[s], src_peer(d)) for d in (1, 2, 3)]
 
     def spread(x, frames):
         block = x.at[frames, 0:5, own]
-        return [remote(block, block, src_peer(d)) for d in (1, 2, 3)]
+        return [remote(block, block, src_peer(d)) for d in (1, 3)]
+
+    def relay(x, frames):
+        copies = []
+        for d, first in ((1, 0), (3, 48)):
+            part = pl.ds(pl.multiple_of(lax.rem(s + 4 - d, 4) * 96 + first, 16), 48)
+            block = x.at[frames, 0:5, part]
+            copies.append(remote(block, block, src_peer(d)))
+        return copies
 
     def halo(x, frames):
         return [
@@ -189,14 +213,22 @@
             remote(x.at[frames, 3:5], x.at[frames, 7:9], at_tile(prv)),
         ]
 
-    c1.wait()
-    pack_cache(stage1, x1)
+    cached1 = spread(x1, pl.ds(0, 2))
+    mine = win.at[core, s]
+    params += [remote(mine, mine, src_peer(d)) for d in (1, 2, 3)]
     arrived(step0)
     mine = rows_all.at[pl.ds(base, 4)]
     step1 = [remote(mine, mine, plane_peer(k)) for k in range(15)]
-    cached1 = spread(x1, pl.ds(0, 2))
     c2.wait()
     pack_cache(stage2, x2)
+    place_of, slot_of = iota((128, 2048), 0), iota((128, 2048), 1) // 16
+    held = (lax.rem(slot_of, 4) * 32) + lax.rem(slot_of // 4, 16) * 2 + slot_of // 64
+    holds = jnp.where(place_of == held, 1.0, 0.0).astype(BF16)
+    image_rows = jnp.broadcast_to(map_ref[...].astype(F32), (8, 128)).astype(BF16)
+    row_at = dot(image_rows, holds)[0:1].astype(jnp.int32)
+    wanted = jnp.clip(tile * 4 - 2 + iota((128, 2048), 0) // 16, 0, 127)
+    same = lax.rem(iota((128, 2048), 0), 16) == lax.rem(iota((128, 2048), 1), 16)
+    choice[...] = jnp.where((row_at == wanted) & same, 1.0, 0.0).astype(BF16)
 
     wide_from, wide_to = iota((160, 256), 0), iota((160, 256), 1)
     shift = jnp.concatenate(
@@ -214,16 +246,21 @@
     for f in range(2):
         put_shifted(f, dot(lcache[f].reshape(128, 160), shift))
 
+    arrived(cached1)
     arrived(step1)
     half = rows_all.at[pl.ds(pl.multiple_of(core * 64, 64), 64)]
     step2 = [remote(half, half, other)]
+    cached1 = relay(x1, pl.ds(0, 2))
     arrived(step2)
-    for j in range(8):
-        picked[s, j] = rows_all[index_ref[j]]
+    chosen = dot(choice[...], rows_all[...].reshape(2048, 128))
+    picked[s] = chosen.astype(BF16).reshape(8, 16, 128)
     step3 = [remote(picked.at[s], picked.at[s], src_peer(d)) for d in (1, 2, 3)]
+    cached2 = spread(x2, pl.ds(0, 2))
     arrived(params)
+    params = [remote(win.at[core], win.at[core], other)]
     arrived(step3)
-    cached2 = spread(x2, pl.ds(0, 2))
+    arrived(cached1)
+    rims = halo(x1, pl.ds(0, 2))
     tail_from, tail_to = iota((128, 256), 0), iota((128, 256), 1)
     for f in range(3):
         tail_shift = []
@@ -236,10 +273,14 @@
         )
         put_shifted(2 + f, wide)
 
+    arrived(params)
     lane = iota((384, 128), 1)
     lane96 = iota((96, 128), 1)
     sum1[...] = jnp.zeros_like(sum1)
     sum2[...] = jnp.zeros_like(sum2)
+
+    def all_taps():
+        return jnp.concatenate([win[i % 2, i // 2] for i in range(8)], axis=0)
 
     @pl.loop(0, 3)
     def _(t):
@@ -248,7 +289,7 @@
             window = jnp.concatenate(
                 [shifted[t + a, h : h + 3].reshape(144, 256) for a in range(3)], axis=0
             )
-            got = dot(win[...], window)
+            got = dot(all_taps(), window)
             first = got[:, 0:128].astype(BF16)
             x1[t + 2, SLOT_OF[h]] = first
             ends = got[:, 128:256]
@@ -286,17 +327,19 @@
         rb = dot_exact(ones, b, ((1,), (1,)))
         return ra, rb
 
-    def share_stats(k):
-        mine = stat.at[k, core, plane]
+    def share_ring(k, peers_):
+        mine = stat_ring.at[k, s, core]
+        return [remote(mine, mine, ring_peer(i)) for i in peers_]
+
+    def share_plane(k):
+        mine = stat.at[k, plane]
         return [remote(mine, mine, plane_peer(i)) for i in range(15)]
 
-    def share_core(k):
-        total = stat[k, core, 0]
+    def plane_total(k):
+        total = stat[k, 0]
         for i in range(1, 16):
-            total = total + stat[k, core, i]
-        stat_core[k, core] = total
-        mine = stat_core.at[k, core]
-        return [remote(mine, mine, other)]
+            total = total + stat[k, i]
+        return total
 
     def coefficients(total, column):
         mean = total / entries
@@ -307,7 +350,15 @@
         mean_c = jnp.sum(one * mean[0:1], axis=1, keepdims=True)
         rstd_c = jnp.sum(one * rstd[0:1], axis=1, keepdims=True)
         mean_ref[...] = jnp.broadcast_to(mean_c, (384, 128))
-        scale = rstd_c * gains[:, column : column + 1] * 0.5
+        eye32 = jnp.where(lane96 == iota((96, 128), 0), 1.0, 0.0)
+        gain_c = jnp.concatenate(
+            [
+                jnp.sum(eye32 * gains[i, column : column + 1], axis=1, keepdims=True)
+                for i in range(4)
+            ],
+            axis=0,
+        )
+        scale = rstd_c * gain_c * 0.5
         scale_ref[...] = jnp.broadcast_to(scale, (384, 128))
 
     def prepare(x, t, f, norm):
@@ -347,8 +398,7 @@
             t[f, 0, part] = pltpu.roll(jnp.where(lane96 >= 96, rim, mid), 32, 1).astype(BF16)
             t[f, 2, part] = pltpu.roll(jnp.where(lane96 < 32, rim, mid), 96, 1).astype(BF16)
 
-    def conv_frame(x, t, w, f):
-        low, high = max(0, f - 2), min(2, f)
+    def conv_frame(x, t, w, f, low, high):
         count = high - low + 1
         taps = w[low : high + 1].reshape(count * 288, 1152)
 
@@ -388,30 +438,34 @@
         return mains, a(4, 1) + left + right
 
     ra, rb = stat_row(sum1[...], sum2[...], 384)
-    stat[0, core, plane] = dot_exact(ra, member(0), ((1,), (0,))) + dot_exact(
+    stat_ring[0, s, core] = dot_exact(ra, member(0), ((1,), (0,))) + dot_exact(
         rb, member(32), ((1,), (0,))
     )
-    shared = share_stats(0)
-    arrived(cached1)
-    rims = halo(x1, pl.ds(0, 2))
-    arrived(shared)
-    shared = share_core(0)
+    shared = share_ring(0, (3,))
     for c in wl1:
         c.wait()
     arrived(rims)
-    prepare(x1, t1, 0, False)
-    prepare(x1, t1, 1, False)
-    conv_frame(x1, t1, w1, 0)
-    conv_frame(x1, t1, w1, 1)
     arrived(shared)
-    coefficients(stat_core[0, 0] + stat_core[0, 1], 0)
+    stat[0, plane] = stat_ring[0, s, 0] + stat_ring[0, s, 1]
+    shared = share_plane(0)
+    for f in range(2):
+        prepare(x1, t1, f, False)
+        conv_frame(x1, t1, w1, f, 0, f)
+    arrived(cached2)
+    cached2 = relay(x2, pl.ds(0, 2))
+    arrived(shared)
+    coefficients(plane_total(0), 0)
 
     total1 = jnp.zeros((96, 128), F32)
     total2 = jnp.zeros((96, 128), F32)
     middles = []
     for t in range(3):
         prepare(x1, t1, t + 2, True)
-        conv_frame(x1, t1, w1, t + 2)
+        if t == 1:
+            conv_frame(x1, t1, w1, 2, 0, 1)
+        if t == 2:
+            conv_frame(x1, t1, w1, 3, 1, 1)
+        conv_frame(x1, t1, w1, t + 2, 2, 2)
         mains, tail = combined(t)
         for h in range(4):
             x2[t + 2, ROW_SLOT[h], own] = mains[h].astype(BF16)
@@ -420,53 +474,62 @@
             total1 = total1 + v
             total2 = total2 + v * v
         middles.append(spread(x2, t + 2))
-
-    ones = jnp.ones((8, 128), F32)
+        if t == 0:
+            arrived(cached2)
+            rims2 = halo(x2, pl.ds(0, 2))
+
     sum1[...] = jnp.zeros_like(sum1)
     sum2[...] = jnp.zeros_like(sum2)
     sum1[own] = total1
     sum2[own] = total2
     ra, rb = stat_row(sum1[...], sum2[...], 384)
-    stat[1, core, plane] = dot_exact(ra, member(0), ((1,), (0,))) + dot_exact(
+    stat_ring[1, s, core] = dot_exact(ra, member(0), ((1,), (0,))) + dot_exact(
         rb, member(32), ((1,), (0,))
     )
-    shared = share_stats(1)
-    arrived(cached2)
-    rims2 = halo(x2, pl.ds(0, 2))
-    arrived(shared)
-    shared = share_core(1)
+    shared = share_ring(1, range(7))
     for c in wl2:
         c.wait()
     arrived(rims2)
-    prepare(x2, t2, 0, False)
+    for f in range(2):
+        prepare(x2, t2, f, False)
+    conv_frame(x2, t2, w2, 0, 0, 0)
+    arrived(middles[0])
+    middles[0] = relay(x2, 2)
     arrived(shared)
-    stat_src[s] = stat_core[1, 0] + stat_core[1, 1]
-    shared = [remote(stat_src.at[s], stat_src.at[s], src_peer(d)) for d in (1, 2, 3)]
+    total = stat_ring[1, 0, 0] + stat_ring[1, 0, 1]
+    for i in range(1, 4):
+        total = total + (stat_ring[1, i, 0] + stat_ring[1, i, 1])
+    stat[1, plane] = total
+    shared = share_plane(1)
+    arrived(middles[1])
+    middles[1] = relay(x2, 3)
+    conv_frame(x2, t2, w2, 1, 0, 1)
     arrived(middles[0])
     rims = [halo(x2, 2)]
-    prepare(x2, t2, 1, False)
-    conv_frame(x2, t2, w2, 0)
-    arrived(middles[1])
-    rims.append(halo(x2, 3))
-    conv_frame(x2, t2, w2, 1)
+    arrived(middles[2])
+    middles[2] = relay(x2, 4)
     arrived(shared)
-    coefficients(stat_src[0] + stat_src[1] + stat_src[2] + stat_src[3], 1)
+    coefficients(plane_total(1), 1)
+    eye128 = jnp.where(iota((128, 128), 0) == iota((128, 128), 1), 1.0, 0.0).astype(BF16)
     for t in range(3):
         arrived(rims[t])
         gone()
         prepare(x2, t2, t + 2, True)
-        conv_frame(x2, t2, w2, t + 2)
+        if t == 0:
+            arrived(middles[1])
+            rims.append(halo(x2, 3))
+        conv_frame(x2, t2, w2, t + 2, t, 2)
         if t == 0:
             arrived(middles[2])
             rims.append(halo(x2, 4))
         mains, tail = combined(t)
         for h in range(4):
-            out = kept[t, ROW_SLOT[h]].astype(F32) + mains[h]
-            out_ref[t, h, :, 0:128] = out.astype(BF16)
-        out = kept[t, TAIL].astype(F32) + tail
+            out = (kept[t, ROW_SLOT[h]].astype(F32) + mains[h]).astype(BF16)
+            out_ref[t, h, 0:128] = dot_t(eye128, out).astype(BF16)
+        out = (kept[t, TAIL].astype(F32) + tail).astype(BF16)
+        turned = dot_t(eye128, out).astype(BF16)
         for h in range(4):
-            moved = out if h == 0 else pltpu.roll(out, 128 - 32 * h, 1)
-            out_ref[t, h, :, 128:160] = moved[:, 0:32].astype(BF16)
+            out_ref[t, h, 128:160] = turned[32 * h : 32 * h + 32]
     gone()
 
 
@@ -483,25 +546,14 @@
     gain_two,
 ):
     frames, _, channels_in, columns = latent.shape
-    tile = lax.axis_index(TILE)
-    wanted = jnp.clip(tile * 4 - 2 + jnp.arange(8, dtype=jnp.int32), 0, 127)
-    places = jnp.arange(128, dtype=jnp.int32)
-    t = places % 32
-    slot = (t % 2) * 64 + (t // 2) * 4 + places // 32
-    index = jnp.sum(
-        jnp.where(row_map[None, :] == wanted[:, None], slot[None, :], 0), axis=1, dtype=jnp.int32
-    )
-    win = conv_in_w.reshape(27 * channels_in, -1).T
-    gains = jnp.pad(jnp.stack([gain_one, gain_two], axis=1), ((0, 0), (0, 126)))
     entries = float(frames * 128 * GSIZE * columns)
     vmem = pl.BlockSpec(memory_space=pltpu.VMEM)
     hbm = pl.BlockSpec(memory_space=pl.ANY)
-    smem = pl.BlockSpec(memory_space=pltpu.SMEM)
-    copies = 3 + 2 + 6 + 15 + 1 + 3 + 3 + 3 + 15 + 2 + 1 + 9 + 15 + 2 + 1 + 3 + 6
-    return pl.pallas_call(
+    copies = 3 + 2 + 7 + 15 + 1 + 3 + 4 + 4 + 2 + 1 + 15 + 12 + 2 + 7 + 15 + 6
+    decoded = pl.pallas_call(
         functools.partial(body, entries),
-        out_shape=jax.ShapeDtypeStruct((3, 4, 96, 160), BF16),
-        in_specs=[smem, vmem, vmem, vmem, vmem, hbm, hbm, hbm, hbm],
+        out_shape=jax.ShapeDtypeStruct((3, 4, 160, 96), BF16),
+        in_specs=[vmem, vmem, vmem, vmem, vmem, vmem, hbm, hbm, hbm, hbm],
         out_specs=vmem,
         scratch_shapes=[
             pltpu.VMEM((4, 16, 128), BF16),
@@ -509,10 +561,11 @@
             pltpu.VMEM((4, 8, 16, 128), BF16),
             pltpu.VMEM((2, 8, 16, 160), BF16),
             pltpu.VMEM((5, 8, 48, 256), BF16),
-            pltpu.VMEM((384, 432), BF16),
-            pltpu.VMEM((384, 128), F32),
-            pltpu.VMEM((2, 4, 96, 160), BF16),
-            pltpu.VMEM((2, 4, 96, 160), BF16),
+            pltpu.VMEM((2, 4, 48, 432), BF16),
+            pltpu.VMEM((4, 8, 128), F32),
+            pltpu.VMEM((128, 2048), BF16),
+            pltpu.VMEM((2, 4, 160, 96), BF16),
+            pltpu.VMEM((2, 4, 160, 96), BF16),
             pltpu.VMEM((3, 3, 96, 1152), BF16),
             pltpu.VMEM((3, 3, 96, 1152), BF16),
             pltpu.VMEM((5, 9, 384, 128), BF16),
@@ -525,9 +578,8 @@
             pltpu.VMEM((384, 128), F32),
             pltpu.VMEM((384, 128), F32),
             pltpu.VMEM((384, 128), F32),
-            pltpu.VMEM((2, 2, 16, 8, 128), F32),
-            pltpu.VMEM((2, 2, 8, 128), F32),
-            pltpu.VMEM((4, 8, 128), F32),
+            pltpu.VMEM((2, 16, 8, 128), F32),
+            pltpu.VMEM((2, 4, 2, 8, 128), F32),
             pltpu.SemaphoreType.DMA((copies,)),
             pltpu.SemaphoreType.DMA((copies,)),
             pltpu.SemaphoreType.DMA((8,)),
@@ -536,16 +588,18 @@
             collective_id=0, has_side_effects=True, vmem_limit_bytes=56 << 20
         ),
     )(
-        index,
+        row_map.reshape(1, 128),
         latent.reshape(frames, channels_in, columns),
         latent_cache,
-        win,
-        gains,
-        cache_one,
-        cache_two,
+        conv_in_w.reshape(27 * channels_in, 96),
+        gain_one.reshape(1, 96),
+        gain_two.reshape(1, 96),
+        jnp.swapaxes(cache_one, 2, 3),
+        jnp.swapaxes(cache_two, 2, 3),
         weight_one,
         weight_two,
     )
+    return jnp.swapaxes(decoded, 2, 3)
 
 
 def solution(mesh):

time: 91.4 us -> 73.4 us (0.80)
  Pallas kernels: 80.7 us -> 71.3 us
  local copies, waits for them, and re-layouts: 8.3 us -> 1.84 us
  other arithmetic: 2.11 us -> 0 us
    pallas_call x1, Pallas kernels: 80.7 us -> 71.3 us  [per_device(): pl.pallas_call(functools.partial(body, entries), out_shape=jax.ShapeDtype...]
    pallas_call x1 -> x0, local copies, waits for them, and re-layouts: 2.1 us -> none  [per_device(): pl.pallas_call(functools.partial(body, entries), out_shape=jax.ShapeDtype...]
    unnamed x2 -> x1, local copies, waits for them, and re-layouts: 3.83 us -> 1.84 us
    reshape x1 -> x0, local copies, waits for them, and re-layouts: 1.63 us -> none  [per_device(): win = conv_in_w.reshape(27 * channels_in, -1).T]
    reduce_sum x1 -> x0, other arithmetic: 1.42 us -> none  [per_device(): jnp.sum(jnp.where(row_map[None, :] == wanted[:, None], slot[None, :], 0),...]
where the time goes in v1:
time: 73.4 us; the launch traced here: 73.2 us
  Pallas kernels  71.3 us (97%)
  local copies, waits for them, and re-layouts  1.84 us (3%)
    pallas_call x1, Pallas kernels, per_device(): pl.pallas_call(functools.partial(body, entries), out_shape=jax.ShapeDtype...  71.3 us
    unnamed x1, local copies, waits for them, and re-layouts  1.84 us

profile of v1, /device:TPU:0, one launch (start us, length us, event | category | flops | bytes accessed | tf_op | source)
XLA Modules:
  0.0 73.2 jit_solution(5698830300829018572)
XLA Ops:
  0.0 71.3 %shard_map.100 = bf16[3,4,160,96]{3,2,1,0:T(8,128)(2,1)} custom-call(s32[1,128]{1,0:T(1,128)} %bitcast.13, bf16[3,16,160]{2,1,0:T(8,128)(2,1)} %bitcast.12, bf16[2,4,16,160]{3,2,1,0:T(8,128)(2,1)} %lcache_ref.1, bf16[432,96]{1,0:T(8,128)(2,1)} %bitcast.11, f32[1,96]{1,0:T(1,128)} %bitcast.14, f32[1,96]{1,0:T(1,128)} %bitcast.15, ...), custom_call_target="tpu_custom_call" | custom-call | tf_op jit(solution)/shard_map/pallas_call | solution.py:553
  71.3 1.8 %copy.12 = bf16[3,4,96,160]{2,3,1,0:T(8,128)(2,1)} copy(bf16[3,4,96,160]{2,3,1,0:T(8,128)(2,1)} %bitcast.8) | data formatting | bytes 737280

commit v2 on v1

--- a/solution.py
+++ b/solution.py
@@ -107,10 +107,12 @@
 
     counter = [0]
 
-    def remote(src, dst, device):
-        k = counter[0]
-        counter[0] += 1
-        c = pltpu.make_async_remote_copy(
+    def taken(count):
+        counter[0] += count
+        return counter[0] - count
+
+    def copy_of(k, src, dst, device):
+        return pltpu.make_async_remote_copy(
             src_ref=src,
             dst_ref=dst,
             send_sem=send_sem.at[k],
@@ -118,8 +120,14 @@
             device_id=device,
             device_id_type=MESH,
         )
+
+    def remote(src, dst, device):
+        c = copy_of(taken(1), src, dst, device)
         c.start()
         return c
+
+    def remotes(moves):
+        return [remote(*move) for move in moves]
 
     def local(src, dst, k):
         c = pltpu.make_async_copy(src, dst, local_sem.at[k])
@@ -173,6 +181,7 @@
     gains[s] = jnp.zeros((8, 128), F32)
     gains[s, 0:1, 0:96] = gain1_ref[...]
     gains[s, 1:2, 0:96] = gain2_ref[...]
+    acc[...] = jnp.zeros_like(acc)
     for f in range(2):
         lcache[f, 2:6] = lcache_ref[f]
     def pack_cache(staged, x):
@@ -197,23 +206,33 @@
 
     def spread(x, frames):
         block = x.at[frames, 0:5, own]
-        return [remote(block, block, src_peer(d)) for d in (1, 3)]
+        return [(block, block, src_peer(d)) for d in (1, 3)]
 
     def relay(x, frames):
-        copies = []
+        moves = []
         for d, first in ((1, 0), (3, 48)):
             part = pl.ds(pl.multiple_of(lax.rem(s + 4 - d, 4) * 96 + first, 16), 48)
             block = x.at[frames, 0:5, part]
-            copies.append(remote(block, block, src_peer(d)))
-        return copies
+            moves.append((block, block, src_peer(d)))
+        return moves
 
     def halo(x, frames):
         return [
-            remote(x.at[frames, 2:4], x.at[frames, 5:7], at_tile(nxt)),
-            remote(x.at[frames, 3:5], x.at[frames, 7:9], at_tile(prv)),
+            (x.at[frames, 2:4], x.at[frames, 5:7], at_tile(nxt)),
+            (x.at[frames, 3:5], x.at[frames, 7:9], at_tile(prv)),
         ]
 
-    cached1 = spread(x1, pl.ds(0, 2))
+    def block_halo(x, frames, ways):
+        moves = []
+        for d in ways:
+            part = pl.ds(pl.multiple_of(lax.rem(s + d, 4) * 96, 96), 96)
+            moves += [
+                (x.at[frames, 2:4, part], x.at[frames, 5:7, part], at_tile(nxt)),
+                (x.at[frames, 3:5, part], x.at[frames, 7:9, part], at_tile(prv)),
+            ]
+        return moves
+
+    cached1 = remotes(spread(x1, pl.ds(0, 2)))
     mine = win.at[core, s]
     params += [remote(mine, mine, src_peer(d)) for d in (1, 2, 3)]
     arrived(step0)
@@ -250,17 +269,17 @@
     arrived(step1)
     half = rows_all.at[pl.ds(pl.multiple_of(core * 64, 64), 64)]
     step2 = [remote(half, half, other)]
-    cached1 = relay(x1, pl.ds(0, 2))
+    cached1 = remotes(relay(x1, pl.ds(0, 2)))
     arrived(step2)
     chosen = dot(choice[...], rows_all[...].reshape(2048, 128))
     picked[s] = chosen.astype(BF16).reshape(8, 16, 128)
     step3 = [remote(picked.at[s], picked.at[s], src_peer(d)) for d in (1, 2, 3)]
-    cached2 = spread(x2, pl.ds(0, 2))
     arrived(params)
     params = [remote(win.at[core], win.at[core], other)]
     arrived(step3)
+    cached2 = remotes(spread(x2, pl.ds(0, 2)))
     arrived(cached1)
-    rims = halo(x1, pl.ds(0, 2))
+    rims = remotes(halo(x1, pl.ds(0, 2)))
     tail_from, tail_to = iota((128, 256), 0), iota((128, 256), 1)
     for f in range(3):
         tail_shift = []
@@ -282,37 +301,40 @@
     def all_taps():
         return jnp.concatenate([win[i % 2, i // 2] for i in range(8)], axis=0)
 
+    def first_row(t, h):
+        window = jnp.concatenate(
+            [shifted[t + a, h : h + 3].reshape(144, 256) for a in range(3)], axis=0
+        )
+        got = dot(all_taps(), window)
+        first = got[:, 0:128].astype(BF16)
+        x1[t + 2, SLOT_OF[h]] = first
+        return first.astype(F32), got[:, 128:256]
+
     @pl.loop(0, 3)
     def _(t):
         tail = jnp.zeros((384, 128), F32)
-        for h in range(6):
-            window = jnp.concatenate(
-                [shifted[t + a, h : h + 3].reshape(144, 256) for a in range(3)], axis=0
-            )
-            got = dot(all_taps(), window)
-            first = got[:, 0:128].astype(BF16)
-            x1[t + 2, SLOT_OF[h]] = first
-            ends = got[:, 128:256]
-            if h == 0:
-                x1[t + 2, UP_TAIL] = pltpu.roll(ends, 96, 1).astype(BF16)
-            elif h == 5:
-                x1[t + 2, DOWN_TAIL] = ends.astype(BF16)
-            else:
-                if h > 1:
-                    ends = pltpu.roll(ends, 32 * (h - 1), 1)
-                hit = (lane >= 32 * (h - 1)) & (lane < 32 * h)
-                tail = jnp.where(hit, ends, tail)
-                full = first.astype(F32)
-                sum1[...] += full
-                sum2[...] += full * full
+        for h in range(1, 5):
+            full, ends = first_row(t, h)
+            if h > 1:
+                ends = pltpu.roll(ends, 32 * (h - 1), 1)
+            hit = (lane >= 32 * (h - 1)) & (lane < 32 * h)
+            tail = jnp.where(hit, ends, tail)
+            sum1[...] += full
+            sum2[...] += full * full
         tail = tail.astype(BF16)
         x1[t + 2, TAIL] = tail
         full = tail.astype(F32)
         sum1[...] += full
         sum2[...] += full * full
 
-    for t in range(3):
-        kept[t] = x1[t + 2, 0:5, own]
+    def first_rims():
+        @pl.loop(0, 3)
+        def _(t):
+            _, ends = first_row(t, 0)
+            x1[t + 2, UP_TAIL] = pltpu.roll(ends, 96, 1).astype(BF16)
+            _, ends = first_row(t, 5)
+            x1[t + 2, DOWN_TAIL] = ends.astype(BF16)
+
 
     channel, group = iota((384, 128), 0), iota((384, 128), 1)
 
@@ -398,26 +420,27 @@
             t[f, 0, part] = pltpu.roll(jnp.where(lane96 >= 96, rim, mid), 32, 1).astype(BF16)
             t[f, 2, part] = pltpu.roll(jnp.where(lane96 < 32, rim, mid), 96, 1).astype(BF16)
 
-    def conv_frame(x, t, w, f, low, high):
-        count = high - low + 1
-        taps = w[low : high + 1].reshape(count * 288, 1152)
-
-        def add(got, i):
-            for n, a in enumerate(range(low, high + 1)):
-                part = got[n * 288 : (n + 1) * 288]
-                if a == 0:
-                    acc[f - a, i] = part
-                else:
-                    acc[f - a, i] += part
+    def conv_step(x, t, w, f, a):
+        taps = w[a].reshape(288, 1152)
 
         def rows(h):
             return jnp.concatenate([x[f, SLOT_OF[h + b]] for b in range(3)], axis=0)
 
         for p in range(2):
             got = dot(taps, jnp.concatenate([rows(2 * p), rows(2 * p + 1)], axis=1))
-            add(got[:, 0:128], 2 * p)
-            add(got[:, 128:256], 2 * p + 1)
-        add(dot(taps, t[f].reshape(1152, 128)), 4)
+            acc[f - a, 2 * p] += got[:, 0:128]
+            acc[f - a, 2 * p + 1] += got[:, 128:256]
+        acc[f - a, 4] += dot(taps, t[f].reshape(1152, 128))
+
+    def cached_prepare(x, t):
+        @pl.loop(0, 2)
+        def _(f):
+            prepare(x, t, f, False)
+
+    def cached_frames(x, t, w):
+        @pl.loop(0, 3)
+        def _(i):
+            conv_step(x, t, w, jnp.minimum(i, 1), jnp.maximum(i - 1, 0))
 
     def combined(t):
         def a(i, e):
@@ -442,95 +465,150 @@
         rb, member(32), ((1,), (0,))
     )
     shared = share_ring(0, (3,))
+    arrived(shared)
+    stat[0, plane] = stat_ring[0, s, 0] + stat_ring[0, s, 1]
+    shared = share_plane(0)
+    first_rims()
+    for t in range(3):
+        kept[t] = x1[t + 2, 0:5, own]
     for c in wl1:
         c.wait()
     arrived(rims)
-    arrived(shared)
-    stat[0, plane] = stat_ring[0, s, 0] + stat_ring[0, s, 1]
-    shared = share_plane(0)
-    for f in range(2):
-        prepare(x1, t1, f, False)
-        conv_frame(x1, t1, w1, f, 0, f)
+    cached_prepare(x1, t1)
+    cached_frames(x1, t1, w1)
     arrived(cached2)
-    cached2 = relay(x2, pl.ds(0, 2))
+    cached2 = remotes(relay(x2, pl.ds(0, 2)))
     arrived(shared)
     coefficients(plane_total(0), 0)
 
-    total1 = jnp.zeros((96, 128), F32)
-    total2 = jnp.zeros((96, 128), F32)
-    middles = []
-    for t in range(3):
+    sum1[...] = jnp.zeros_like(sum1)
+    sum2[...] = jnp.zeros_like(sum2)
+    first_copy = taken(36)
+
+    def of_frame(first, moves, t):
+        k = first_copy + t * 12 + first
+        return [copy_of(k + i, *move) for i, move in enumerate(moves)]
+
+    def middle_spread(t):
+        return of_frame(0, spread(x2, t + 2), t)
+
+    def middle_relay(t):
+        return of_frame(2, relay(x2, t + 2), t)
+
+    def halo_own(t):
+        return of_frame(4, block_halo(x2, t + 2, (0,)), t)
+
+    def halo_near(t):
+        return of_frame(6, block_halo(x2, t + 2, (1, 3)), t)
+
+    def halo_far(t):
+        return of_frame(10, block_halo(x2, t + 2, (2,)), t)
+
+    def start(copies):
+        for c in copies:
+            c.start()
+
+    def landed(copies):
+        for c in copies:
+            c.wait_recv()
+
+    first_rims2 = taken(2)
+    rims2 = [copy_of(first_rims2 + i, *m) for i, m in enumerate(halo(x2, pl.ds(0, 2)))]
+
+    @pl.loop(0, 3)
+    def _(t):
         prepare(x1, t1, t + 2, True)
-        if t == 1:
-            conv_frame(x1, t1, w1, 2, 0, 1)
-        if t == 2:
-            conv_frame(x1, t1, w1, 3, 1, 1)
-        conv_frame(x1, t1, w1, t + 2, 2, 2)
+
+        @pl.loop(2 - t, 3)
+        def _(a):
+            conv_step(x1, t1, w1, t + a, a)
+
         mains, tail = combined(t)
+        acc[t] = jnp.zeros((5, 288, 128), F32)
+        total1, total2 = sum1[own], sum2[own]
         for h in range(4):
             x2[t + 2, ROW_SLOT[h], own] = mains[h].astype(BF16)
         x2[t + 2, TAIL, own] = tail.astype(BF16)
+        start(middle_spread(t))
+        start(halo_own(t))
         for v in mains + [tail]:
             total1 = total1 + v
             total2 = total2 + v * v
-        middles.append(spread(x2, t + 2))
-        if t == 0:
-            arrived(cached2)
-            rims2 = halo(x2, pl.ds(0, 2))
-
-    sum1[...] = jnp.zeros_like(sum1)
-    sum2[...] = jnp.zeros_like(sum2)
-    sum1[own] = total1
-    sum2[own] = total2
+        sum1[own] = total1
+        sum2[own] = total2
+
+        @pl.when(t == 1)
+        def _():
+            landed(cached2)
+            start(rims2)
+
+    sent.extend(cached2)
     ra, rb = stat_row(sum1[...], sum2[...], 384)
     stat_ring[1, s, core] = dot_exact(ra, member(0), ((1,), (0,))) + dot_exact(
         rb, member(32), ((1,), (0,))
     )
     shared = share_ring(1, range(7))
+    landed(middle_spread(0))
+    start(middle_relay(0))
+    start(halo_near(0))
     for c in wl2:
         c.wait()
     arrived(rims2)
-    for f in range(2):
-        prepare(x2, t2, f, False)
-    conv_frame(x2, t2, w2, 0, 0, 0)
-    arrived(middles[0])
-    middles[0] = relay(x2, 2)
     arrived(shared)
     total = stat_ring[1, 0, 0] + stat_ring[1, 0, 1]
     for i in range(1, 4):
         total = total + (stat_ring[1, i, 0] + stat_ring[1, i, 1])
     stat[1, plane] = total
     shared = share_plane(1)
-    arrived(middles[1])
-    middles[1] = relay(x2, 3)
-    conv_frame(x2, t2, w2, 1, 0, 1)
-    arrived(middles[0])
-    rims = [halo(x2, 2)]
-    arrived(middles[2])
-    middles[2] = relay(x2, 4)
+    landed(middle_spread(1))
+    start(middle_relay(1))
+    start(halo_near(1))
+    cached_prepare(x2, t2)
+    landed(middle_relay(0))
+    start(halo_far(0))
+    landed(middle_spread(2))
+    start(middle_relay(2))
+    start(halo_near(2))
+    cached_frames(x2, t2, w2)
+    landed(middle_relay(1))
+    start(halo_far(1))
     arrived(shared)
     coefficients(plane_total(1), 1)
-    eye128 = jnp.where(iota((128, 128), 0) == iota((128, 128), 1), 1.0, 0.0).astype(BF16)
-    for t in range(3):
-        arrived(rims[t])
-        gone()
+    gone()
+
+    @pl.loop(0, 3)
+    def _(t):
+        edges_ = halo_own(t) + halo_near(t) + halo_far(t)
+        landed(edges_)
+        for c in middle_spread(t) + middle_relay(t) + edges_:
+            c.wait_send()
         prepare(x2, t2, t + 2, True)
-        if t == 0:
-            arrived(middles[1])
-            rims.append(halo(x2, 3))
-        conv_frame(x2, t2, w2, t + 2, t, 2)
-        if t == 0:
-            arrived(middles[2])
-            rims.append(halo(x2, 4))
+
+        @pl.when(t == 0)
+        def _():
+            landed(middle_relay(2))
+            start(halo_far(2))
+
+        @pl.loop(2 - t, 3)
+        def _(a):
+            conv_step(x2, t2, w2, t + a, a)
+
         mains, tail = combined(t)
         for h in range(4):
             out = (kept[t, ROW_SLOT[h]].astype(F32) + mains[h]).astype(BF16)
-            out_ref[t, h, 0:128] = dot_t(eye128, out).astype(BF16)
+            out_ref[t, h] = out
         out = (kept[t, TAIL].astype(F32) + tail).astype(BF16)
-        turned = dot_t(eye128, out).astype(BF16)
+        out_ref[t, 4] = out
+
+
+def channels_last(from_ref, to_ref):
+    eye = jnp.where(iota((128, 128), 0) == iota((128, 128), 1), 1.0, 0.0).astype(BF16)
+    for t in range(3):
         for h in range(4):
-            out_ref[t, h, 128:160] = turned[32 * h : 32 * h + 32]
-    gone()
+            to_ref[t, h, 0:128] = dot_t(eye, from_ref[t, h]).astype(BF16)
+        turned = dot_t(eye, from_ref[t, 4]).astype(BF16)
+        for h in range(4):
+            to_ref[t, h, 128:160] = turned[32 * h : 32 * h + 32]
 
 
 def per_device(
@@ -549,10 +627,10 @@
     entries = float(frames * 128 * GSIZE * columns)
     vmem = pl.BlockSpec(memory_space=pltpu.VMEM)
     hbm = pl.BlockSpec(memory_space=pl.ANY)
-    copies = 3 + 2 + 7 + 15 + 1 + 3 + 4 + 4 + 2 + 1 + 15 + 12 + 2 + 7 + 15 + 6
+    copies = 3 + 2 + 7 + 15 + 1 + 3 + 4 + 4 + 2 + 1 + 15 + 36 + 2 + 7 + 15
     decoded = pl.pallas_call(
         functools.partial(body, entries),
-        out_shape=jax.ShapeDtypeStruct((3, 4, 160, 96), BF16),
+        out_shape=jax.ShapeDtypeStruct((3, 5, 96, 128), BF16),
         in_specs=[vmem, vmem, vmem, vmem, vmem, vmem, hbm, hbm, hbm, hbm],
         out_specs=vmem,
         scratch_shapes=[
@@ -599,6 +677,12 @@
         weight_one,
         weight_two,
     )
+    decoded = pl.pallas_call(
+        channels_last,
+        out_shape=jax.ShapeDtypeStruct((3, 4, 160, 96), BF16),
+        in_specs=[vmem],
+        out_specs=vmem,
+    )(decoded)
     return jnp.swapaxes(decoded, 2, 3)
 
 

time: 73.4 us -> 67.8 us (0.924)
  Pallas kernels: 71.3 us -> 67.7 us
  local copies, waits for them, and re-layouts: 1.84 us -> 0 us
    pallas_call x1, Pallas kernels: 71.3 us -> 65.5 us  [per_device(): pl.pallas_call(functools.partial(body, entries), out_shape=jax.ShapeDtype...]
    pallas_call x0 -> x1, Pallas kernels: none -> 2.15 us  [per_device(): pl.pallas_call(channels_last, out_shape=jax.ShapeDtypeStruct((3, 4, 160,...]
    unnamed x1 -> x0, local copies, waits for them, and re-layouts: 1.84 us -> none
where the time goes in v2:
time: 67.8 us; the launch traced here: 67.7 us
  Pallas kernels  67.7 us (100%)
    pallas_call x1, Pallas kernels, per_device(): pl.pallas_call(functools.partial(body, entries), out_shape=jax.ShapeDtype...  65.5 us
    pallas_call x1, Pallas kernels, per_device(): pl.pallas_call(channels_last, out_shape=jax.ShapeDtypeStruct((3, 4, 160,...  2.15 us

profile of v2, /device:TPU:0, one launch (start us, length us, event | category | flops | bytes accessed | tf_op | source)
XLA Modules:
  0.0 67.7 jit_solution(11685923153586361944)
XLA Ops:
  0.0 65.5 %shard_map.100.from_ref = bf16[3,5,96,128]{3,2,1,0:T(8,128)(2,1)} custom-call(s32[1,128]{1,0:T(1,128)} %bitcast.12, bf16[3,16,160]{2,1,0:T(8,128)(2,1)} %bitcast.11, bf16[2,4,16,160]{3,2,1,0:T(8,128)(2,1)} %lcache_ref.1, bf16[432,96]{1,0:T(8,128)(2,1)} %bitcast.10, f32[1,96]{1,0:T(1,128)} %bitcast.13, f32[1,96]{1,0:T(1,128)} %bitcast.14, ...), custom_call_target="tpu_custom_call" | custom-call | tf_op jit(solution)/shard_map/pallas_call | solution.py:631
  65.5 2.2 %shard_map.101 = bf16[3,4,160,96]{3,2,1,0:T(8,128)(2,1)} custom-call(bf16[3,5,96,128]{3,2,1,0:T(8,128)(2,1)} %shard_map.100.from_ref), custom_call_target="tpu_custom_call" | custom-call | tf_op jit(solution)/shard_map/pallas_call | solution.py:680

commit v3 on v2

--- a/solution.py
+++ b/solution.py
@@ -72,8 +72,10 @@
     t2,
     acc,
     kept,
-    sum1,
-    sum2,
+    sums,
+    members,
+    gain_cols,
+    tail_shifts,
     mean_ref,
     scale_ref,
     stat,
@@ -182,6 +184,14 @@
     gains[s, 0:1, 0:96] = gain1_ref[...]
     gains[s, 1:2, 0:96] = gain2_ref[...]
     acc[...] = jnp.zeros_like(acc)
+    sum1, sum2 = sums.at[0:384], sums.at[384:768]
+    channel, group = iota((384, 128), 0), iota((384, 128), 1)
+    for i in range(2):
+        low = (group - 32 * i) * GSIZE
+        hit = (channel >= low) & (channel < low + GSIZE)
+        hit &= (group >= 32 * i) & (group < 32 * i + 32)
+        members[384 * i : 384 * i + 384] = jnp.where(hit, 1.0, 0.0)
+    sums[...] = jnp.zeros_like(sums)
     for f in range(2):
         lcache[f, 2:6] = lcache_ref[f]
     def pack_cache(staged, x):
@@ -215,12 +225,6 @@
             block = x.at[frames, 0:5, part]
             moves.append((block, block, src_peer(d)))
         return moves
-
-    def halo(x, frames):
-        return [
-            (x.at[frames, 2:4], x.at[frames, 5:7], at_tile(nxt)),
-            (x.at[frames, 3:5], x.at[frames, 7:9], at_tile(prv)),
-        ]
 
     def block_halo(x, frames, ways):
         moves = []
@@ -233,6 +237,7 @@
         return moves
 
     cached1 = remotes(spread(x1, pl.ds(0, 2)))
+    rims = remotes(block_halo(x1, pl.ds(0, 2), (0,)))
     mine = win.at[core, s]
     params += [remote(mine, mine, src_peer(d)) for d in (1, 2, 3)]
     arrived(step0)
@@ -261,6 +266,12 @@
             part = wide[:, e * 256 : (e + 1) * 256].reshape(8, 16, 256)
             shifted[f, :, e * 16 : (e + 1) * 16] = jnp.where(in_image, part, 0.0).astype(BF16)
 
+    tail_from, tail_to = iota((128, 256), 0), iota((128, 256), 1)
+    for f in range(3):
+        for e in range(3):
+            j = tail_from - 32 * f
+            hit = (j >= 0) & (j < 32) & (128 + j == tail_to + e - 1)
+            tail_shifts[f, :, 256 * e : 256 * e + 256] = jnp.where(hit, 1.0, 0.0).astype(BF16)
     arrived(edges)
     for f in range(2):
         put_shifted(f, dot(lcache[f].reshape(128, 160), shift))
@@ -270,6 +281,7 @@
     half = rows_all.at[pl.ds(pl.multiple_of(core * 64, 64), 64)]
     step2 = [remote(half, half, other)]
     cached1 = remotes(relay(x1, pl.ds(0, 2)))
+    rims += remotes(block_halo(x1, pl.ds(0, 2), (1, 3)))
     arrived(step2)
     chosen = dot(choice[...], rows_all[...].reshape(2048, 128))
     picked[s] = chosen.astype(BF16).reshape(8, 16, 128)
@@ -278,25 +290,18 @@
     params = [remote(win.at[core], win.at[core], other)]
     arrived(step3)
     cached2 = remotes(spread(x2, pl.ds(0, 2)))
-    arrived(cached1)
-    rims = remotes(halo(x1, pl.ds(0, 2)))
-    tail_from, tail_to = iota((128, 256), 0), iota((128, 256), 1)
+    rims2 = remotes(block_halo(x2, pl.ds(0, 2), (0,)))
     for f in range(3):
-        tail_shift = []
-        for e in range(3):
-            j = tail_from - 32 * f
-            hit = (j >= 0) & (j < 32) & (128 + j == tail_to + e - 1)
-            tail_shift.append(jnp.where(hit, 1.0, 0.0).astype(BF16))
         wide = dot(picked[f].reshape(128, 128), shift[0:128]) + dot(
-            picked[3].reshape(128, 128), jnp.concatenate(tail_shift, axis=1)
+            picked[3].reshape(128, 128), tail_shifts[f]
         )
         put_shifted(2 + f, wide)
+    arrived(cached1)
+    rims += remotes(block_halo(x1, pl.ds(0, 2), (2,)))
 
     arrived(params)
     lane = iota((384, 128), 1)
     lane96 = iota((96, 128), 1)
-    sum1[...] = jnp.zeros_like(sum1)
-    sum2[...] = jnp.zeros_like(sum2)
 
     def all_taps():
         return jnp.concatenate([win[i % 2, i // 2] for i in range(8)], axis=0)
@@ -336,18 +341,9 @@
             x1[t + 2, DOWN_TAIL] = ends.astype(BF16)
 
 
-    channel, group = iota((384, 128), 0), iota((384, 128), 1)
-
-    def member(first_lane):
-        low = (group - first_lane) * GSIZE
-        hit = (channel >= low) & (channel < low + GSIZE)
-        return jnp.where(hit & (group >= first_lane) & (group < first_lane + 32), 1.0, 0.0)
-
-    def stat_row(a, b, rows):
-        ones = jnp.ones((8, 128), F32)
-        ra = dot_exact(ones, a, ((1,), (1,)))
-        rb = dot_exact(ones, b, ((1,), (1,)))
-        return ra, rb
+    def group_sums():
+        rows = dot_exact(jnp.ones((8, 128), F32), sums[...], ((1,), (1,)))
+        return dot_exact(rows, members[...], ((1,), (0,)))
 
     def share_ring(k, peers_):
         mine = stat_ring.at[k, s, core]
@@ -368,20 +364,18 @@
         square = pltpu.roll(mean, 96, 1)
         spread_ = jnp.maximum(square - mean * mean, 0.0)
         rstd = lax.rsqrt(spread_ + 1e-06)
-        one = member(0)
+        one = members[0:384]
         mean_c = jnp.sum(one * mean[0:1], axis=1, keepdims=True)
         rstd_c = jnp.sum(one * rstd[0:1], axis=1, keepdims=True)
         mean_ref[...] = jnp.broadcast_to(mean_c, (384, 128))
-        eye32 = jnp.where(lane96 == iota((96, 128), 0), 1.0, 0.0)
-        gain_c = jnp.concatenate(
-            [
-                jnp.sum(eye32 * gains[i, column : column + 1], axis=1, keepdims=True)
-                for i in range(4)
-            ],
-            axis=0,
-        )
-        scale = rstd_c * gain_c * 0.5
-        scale_ref[...] = jnp.broadcast_to(scale, (384, 128))
+        scale_ref[...] = jnp.broadcast_to(rstd_c, (384, 128)) * gain_cols[column]
+
+    def gain_columns():
+        unit = jnp.where(lane96 == iota((96, 128), 0), 0.5, 0.0)
+        for column in range(2):
+            for i in range(4):
+                col = jnp.sum(unit * gains[i, column : column + 1], axis=1, keepdims=True)
+                gain_cols[column, 96 * i : 96 * i + 96] = jnp.broadcast_to(col, (96, 128))
 
     def prepare(x, t, f, norm):
         no_up = jnp.where(tile == 0, 128, 0)
@@ -389,7 +383,7 @@
         down_limit = jnp.where(tile == 31, 32, 0)
         up_limit = jnp.where(tile == 0, 96, 128)
 
-        @pl.loop(0, 4)
+        @pl.loop(0, 4, unroll=True)
         def _(c):
             part = pl.ds(pl.multiple_of(c * 96, 96), 96)
             mean, scale = mean_ref[part], scale_ref[part]
@@ -432,6 +426,25 @@
             acc[f - a, 2 * p + 1] += got[:, 128:256]
         acc[f - a, 4] += dot(taps, t[f].reshape(1152, 128))
 
+    def conv_taps(x, t, w, f, low, count):
+        taps = w[low : low + count].reshape(count * 288, 1152)
+
+        def rows(h):
+            return jnp.concatenate([x[f, SLOT_OF[h + b]] for b in range(3)], axis=0)
+
+        for p in range(3):
+            if p < 2:
+                got = dot(taps, jnp.concatenate([rows(2 * p), rows(2 * p + 1)], axis=1))
+            else:
+                got = dot(taps, t[f].reshape(1152, 128))
+            for n in range(count):
+                part = got[n * 288 : (n + 1) * 288]
+                if p < 2:
+                    acc[f - low - n, 2 * p] += part[:, 0:128]
+                    acc[f - low - n, 2 * p + 1] += part[:, 128:256]
+                else:
+                    acc[f - low - n, 4] += part
+
     def cached_prepare(x, t):
         @pl.loop(0, 2)
         def _(f):
@@ -460,14 +473,12 @@
         right = jnp.where((lane96 & 31) == 31, 0.0, pltpu.roll(a(4, 2), 127, 1))
         return mains, a(4, 1) + left + right
 
-    ra, rb = stat_row(sum1[...], sum2[...], 384)
-    stat_ring[0, s, core] = dot_exact(ra, member(0), ((1,), (0,))) + dot_exact(
-        rb, member(32), ((1,), (0,))
-    )
+    stat_ring[0, s, core] = group_sums()
     shared = share_ring(0, (3,))
     arrived(shared)
     stat[0, plane] = stat_ring[0, s, 0] + stat_ring[0, s, 1]
     shared = share_plane(0)
+    gain_columns()
     first_rims()
     for t in range(3):
         kept[t] = x1[t + 2, 0:5, own]
@@ -478,11 +489,11 @@
     cached_frames(x1, t1, w1)
     arrived(cached2)
     cached2 = remotes(relay(x2, pl.ds(0, 2)))
+    rims2 += remotes(block_halo(x2, pl.ds(0, 2), (1, 3)))
     arrived(shared)
     coefficients(plane_total(0), 0)
 
-    sum1[...] = jnp.zeros_like(sum1)
-    sum2[...] = jnp.zeros_like(sum2)
+    sums[...] = jnp.zeros_like(sums)
     first_copy = taken(36)
 
     def of_frame(first, moves, t):
@@ -512,8 +523,10 @@
         for c in copies:
             c.wait_recv()
 
-    first_rims2 = taken(2)
-    rims2 = [copy_of(first_rims2 + i, *m) for i, m in enumerate(halo(x2, pl.ds(0, 2)))]
+    first_far2 = taken(2)
+    far2 = [
+        copy_of(first_far2 + i, *m) for i, m in enumerate(block_halo(x2, pl.ds(0, 2), (2,)))
+    ]
 
     @pl.loop(0, 3)
     def _(t):
@@ -540,20 +553,17 @@
         @pl.when(t == 1)
         def _():
             landed(cached2)
-            start(rims2)
+            start(far2)
 
     sent.extend(cached2)
-    ra, rb = stat_row(sum1[...], sum2[...], 384)
-    stat_ring[1, s, core] = dot_exact(ra, member(0), ((1,), (0,))) + dot_exact(
-        rb, member(32), ((1,), (0,))
-    )
+    stat_ring[1, s, core] = group_sums()
     shared = share_ring(1, range(7))
     landed(middle_spread(0))
     start(middle_relay(0))
     start(halo_near(0))
     for c in wl2:
         c.wait()
-    arrived(rims2)
+    arrived(rims2 + far2)
     arrived(shared)
     total = stat_ring[1, 0, 0] + stat_ring[1, 0, 1]
     for i in range(1, 4):
@@ -589,9 +599,17 @@
             landed(middle_relay(2))
             start(halo_far(2))
 
-        @pl.loop(2 - t, 3)
-        def _(a):
-            conv_step(x2, t2, w2, t + a, a)
+        @pl.when(t == 0)
+        def _():
+            conv_taps(x2, t2, w2, 2, 0, 3)
+
+        @pl.when(t == 1)
+        def _():
+            conv_taps(x2, t2, w2, 3, 1, 2)
+
+        @pl.when(t == 2)
+        def _():
+            conv_taps(x2, t2, w2, 4, 2, 1)
 
         mains, tail = combined(t)
         for h in range(4):
@@ -627,7 +645,7 @@
     entries = float(frames * 128 * GSIZE * columns)
     vmem = pl.BlockSpec(memory_space=pltpu.VMEM)
     hbm = pl.BlockSpec(memory_space=pl.ANY)
-    copies = 3 + 2 + 7 + 15 + 1 + 3 + 4 + 4 + 2 + 1 + 15 + 36 + 2 + 7 + 15
+    copies = 3 + 2 + 7 + 15 + 1 + 3 + 4 + 4 + 8 + 1 + 15 + 36 + 8 + 7 + 15
     decoded = pl.pallas_call(
         functools.partial(body, entries),
         out_shape=jax.ShapeDtypeStruct((3, 5, 96, 128), BF16),
@@ -652,8 +670,10 @@
             pltpu.VMEM((5, 3, 384, 128), BF16),
             pltpu.VMEM((3, 5, 288, 128), F32),
             pltpu.VMEM((3, 5, 96, 128), BF16),
-            pltpu.VMEM((384, 128), F32),
-            pltpu.VMEM((384, 128), F32),
+            pltpu.VMEM((768, 128), F32),
+            pltpu.VMEM((768, 128), F32),
+            pltpu.VMEM((2, 384, 128), F32),
+            pltpu.VMEM((3, 128, 768), BF16),
             pltpu.VMEM((384, 128), F32),
             pltpu.VMEM((384, 128), F32),
             pltpu.VMEM((2, 16, 8, 128), F32),

time: 67.8 us -> 64.2 us (0.947)
  Pallas kernels: 67.7 us -> 64.1 us
    pallas_call x1, Pallas kernels: 65.5 us -> 61.9 us  [per_device(): pl.pallas_call(functools.partial(body, entries), out_shape=jax.ShapeDtype...]
where the time goes in v3:
time: 64.2 us; the launch traced here: 64.1 us
  Pallas kernels  64.1 us (100%)
    pallas_call x1, Pallas kernels, per_device(): pl.pallas_call(functools.partial(body, entries), out_shape=jax.ShapeDtype...  61.9 us
    pallas_call x1, Pallas kernels, per_device(): pl.pallas_call(channels_last, out_shape=jax.ShapeDtypeStruct((3, 4, 160,...  2.15 us

profile of v3, /device:TPU:0, one launch (start us, length us, event | category | flops | bytes accessed | tf_op | source)
XLA Modules:
  0.0 64.1 jit_solution(11340679605954699060)
XLA Ops:
  0.0 61.9 %shard_map.100.from_ref = bf16[3,5,96,128]{3,2,1,0:T(8,128)(2,1)} custom-call(s32[1,128]{1,0:T(1,128)} %bitcast.12, bf16[3,16,160]{2,1,0:T(8,128)(2,1)} %bitcast.11, bf16[2,4,16,160]{3,2,1,0:T(8,128)(2,1)} %lcache_ref.1, bf16[432,96]{1,0:T(8,128)(2,1)} %bitcast.10, f32[1,96]{1,0:T(1,128)} %bitcast.13, f32[1,96]{1,0:T(1,128)} %bitcast.14, ...), custom_call_target="tpu_custom_call" | custom-call | tf_op jit(solution)/shard_map/pallas_call | solution.py:649
  61.9 2.2 %shard_map.101 = bf16[3,4,160,96]{3,2,1,0:T(8,128)(2,1)} custom-call(bf16[3,5,96,128]{3,2,1,0:T(8,128)(2,1)} %shard_map.100.from_ref), custom_call_target="tpu_custom_call" | custom-call | tf_op jit(solution)/shard_map/pallas_call | solution.py:700

commit v4 on v3

--- a/solution.py
+++ b/solution.py
@@ -20,7 +20,12 @@
 TAIL, UP_MAIN, UP_TAIL, DOWN_TAIL, DOWN_MAIN = 3, 5, 6, 7, 8
 ROW_SLOT = (4, 0, 1, 2)
 SLOT_OF = (UP_MAIN, 4, 0, 1, 2, DOWN_MAIN)
-PLANE = tuple((z, y) for z in range(4) for y in range(4) if z or y)
+PLANE = tuple(
+    sorted(
+        ((z, y) for z in range(4) for y in range(4) if z or y),
+        key=lambda step: -sum(min(n, 4 - n) for n in step),
+    )
+)
 
 
 def dot(a, b):
@@ -149,8 +154,8 @@
         sent.clear()
 
     barrier = pltpu.get_barrier_semaphore()
-    peers = [src_peer(d) for d in (1, 2, 3)] + [plane_peer(k) for k in range(15)]
-    peers += [ring_peer(i) for i in range(3, 7)] + [at_tile(nxt), at_tile(prv)]
+    peers = [plane_peer(k) for k in range(15)] + [src_peer(d) for d in (2, 1, 3)]
+    peers += [at_tile(nxt), at_tile(prv)] + [ring_peer(i) for i in (5, 4, 6, 3)]
     for p in peers:
         pl.semaphore_signal(barrier, inc=1, device_id=p, device_id_type=MESH)
     c1 = local(cache1_hbm, stage1, 0)
@@ -206,7 +211,7 @@
     pl.semaphore_wait(barrier, len(peers))
 
     step0 = [
-        remote(units.at[lax.rem(s + d, 4)], rows_all.at[base + s], src_peer(d)) for d in (1, 2, 3)
+        remote(units.at[lax.rem(s + d, 4)], rows_all.at[base + s], src_peer(d)) for d in (2, 1, 3)
     ]
     edges = [
         remote(lcache_ref.at[:, 2:4], lcache.at[:, 0:2], at_tile(nxt)),
@@ -285,7 +290,7 @@
     arrived(step2)
     chosen = dot(choice[...], rows_all[...].reshape(2048, 128))
     picked[s] = chosen.astype(BF16).reshape(8, 16, 128)
-    step3 = [remote(picked.at[s], picked.at[s], src_peer(d)) for d in (1, 2, 3)]
+    step3 = [remote(picked.at[s], picked.at[s], src_peer(d)) for d in (2, 1, 3)]
     arrived(params)
     params = [remote(win.at[core], win.at[core], other)]
     arrived(step3)
@@ -557,7 +562,7 @@
 
     sent.extend(cached2)
     stat_ring[1, s, core] = group_sums()
-    shared = share_ring(1, range(7))
+    shared = share_ring(1, (5, 1, 4, 6, 0, 2, 3))
     landed(middle_spread(0))
     start(middle_relay(0))
     start(halo_near(0))

time: 64.2 us -> 63.4 us (0.988)
  Pallas kernels: 64.1 us -> 63.2 us
    pallas_call x1, Pallas kernels: 61.9 us -> 61.1 us  [per_device(): pl.pallas_call(functools.partial(body, entries), out_shape=jax.ShapeDtype...]
where the time goes in v4:
time: 63.4 us; the launch traced here: 63.2 us
  Pallas kernels  63.2 us (100%)
    pallas_call x1, Pallas kernels, per_device(): pl.pallas_call(functools.partial(body, entries), out_shape=jax.ShapeDtype...  61.1 us
    pallas_call x1, Pallas kernels, per_device(): pl.pallas_call(channels_last, out_shape=jax.ShapeDtypeStruct((3, 4, 160,...  2.16 us

profile of v4, /device:TPU:0, one launch (start us, length us, event | category | flops | bytes accessed | tf_op | source)
XLA Modules:
  0.0 63.2 jit_solution(222031729728805705)
XLA Ops:
  0.0 61.1 %shard_map.100.from_ref = bf16[3,5,96,128]{3,2,1,0:T(8,128)(2,1)} custom-call(s32[1,128]{1,0:T(1,128)} %bitcast.12, bf16[3,16,160]{2,1,0:T(8,128)(2,1)} %bitcast.11, bf16[2,4,16,160]{3,2,1,0:T(8,128)(2,1)} %lcache_ref.1, bf16[432,96]{1,0:T(8,128)(2,1)} %bitcast.10, f32[1,96]{1,0:T(1,128)} %bitcast.13, f32[1,96]{1,0:T(1,128)} %bitcast.14, ...), custom_call_target="tpu_custom_call" | custom-call | tf_op jit(solution)/shard_map/pallas_call | solution.py:654
  61.1 2.2 %shard_map.101 = bf16[3,4,160,96]{3,2,1,0:T(8,128)(2,1)} custom-call(bf16[3,5,96,128]{3,2,1,0:T(8,128)(2,1)} %shard_map.100.from_ref), custom_call_target="tpu_custom_call" | custom-call | tf_op jit(solution)/shard_map/pallas_call | solution.py:705

commit v5 on v4

--- a/solution.py
+++ b/solution.py
@@ -626,12 +626,11 @@
 
 def channels_last(from_ref, to_ref):
     eye = jnp.where(iota((128, 128), 0) == iota((128, 128), 1), 1.0, 0.0).astype(BF16)
-    for t in range(3):
-        for h in range(4):
-            to_ref[t, h, 0:128] = dot_t(eye, from_ref[t, h]).astype(BF16)
-        turned = dot_t(eye, from_ref[t, 4]).astype(BF16)
-        for h in range(4):
-            to_ref[t, h, 128:160] = turned[32 * h : 32 * h + 32]
+    for h in range(4):
+        to_ref[0, h, 0:128] = dot_t(eye, from_ref[0, h]).astype(BF16)
+    turned = dot_t(eye, from_ref[0, 4]).astype(BF16)
+    for h in range(4):
+        to_ref[0, h, 128:160] = turned[32 * h : 32 * h + 32]
 
 
 def per_device(
@@ -705,8 +704,9 @@
     decoded = pl.pallas_call(
         channels_last,
         out_shape=jax.ShapeDtypeStruct((3, 4, 160, 96), BF16),
-        in_specs=[vmem],
-        out_specs=vmem,
+        grid=(3,),
+        in_specs=[pl.BlockSpec((1, 5, 96, 128), lambda t: (t, 0, 0, 0))],
+        out_specs=pl.BlockSpec((1, 4, 160, 96), lambda t: (t, 0, 0, 0)),
     )(decoded)
     return jnp.swapaxes(decoded, 2, 3)
 

time: 63.4 us -> 64.2 us (1.013)
  Pallas kernels: 63.2 us -> 64 us
    pallas_call x1, Pallas kernels: 2.16 us -> 2.97 us  [per_device(): pl.pallas_call(channels_last, out_shape=jax.ShapeDtypeStruct((3, 4, 160,...]
where the time goes in v5:
time: 64.2 us; the launch traced here: 64.1 us
  Pallas kernels  64 us (100%)
    pallas_call x1, Pallas kernels, per_device(): pl.pallas_call(functools.partial(body, entries), out_shape=jax.ShapeDtype...  61.1 us
    pallas_call x1, Pallas kernels, per_device(): pl.pallas_call(channels_last, out_shape=jax.ShapeDtypeStruct((3, 4, 160,...  2.97 us

profile of v5, /device:TPU:0, one launch (start us, length us, event | category | flops | bytes accessed | tf_op | source)
XLA Modules:
  0.0 64.1 jit_solution(5989721222699237023)
XLA Ops:
  0.0 61.1 %shard_map.100.from_ref = bf16[3,5,96,128]{3,2,1,0:T(8,128)(2,1)} custom-call(s32[1,128]{1,0:T(1,128)} %bitcast.12, bf16[3,16,160]{2,1,0:T(8,128)(2,1)} %bitcast.11, bf16[2,4,16,160]{3,2,1,0:T(8,128)(2,1)} %lcache_ref.1, bf16[432,96]{1,0:T(8,128)(2,1)} %bitcast.10, f32[1,96]{1,0:T(1,128)} %bitcast.13, f32[1,96]{1,0:T(1,128)} %bitcast.14, ...), custom_call_target="tpu_custom_call" | custom-call | tf_op jit(solution)/shard_map/pallas_call | solution.py:653
  61.1 3.0 %shard_map.101 = bf16[3,4,160,96]{3,2,1,0:T(8,128)(2,1)} custom-call(bf16[3,5,96,128]{3,2,1,0:T(8,128)(2,1)} %shard_map.100.from_ref), custom_call_target="tpu_custom_call" | custom-call | tf_op jit(solution)/shard_map/pallas_call | solution.py:704
